TPU v7x, 32 devices: a whole 2x2x4 slice. The times are simulated.
32 devices in a mesh: tiles: 32 (over z, y, x, core).
Axes of the slice: x: 2, y: 2, z: 4, core: 2. Of those that a mesh axis runs over, the one named last changes fastest.
Arguments:
- queries: bfloat16 [4096, 1536], P('tiles'), may hold values from -35 to 35
- keys: bfloat16 [4096, 1536], P('tiles'), may hold values from -4.1 to 4.1
- values: bfloat16 [4096, 1536], P('tiles'), may hold values from -4 to 4
- destination: int32 [4096], P('tiles'), may hold values from 0 to 4095, as said below
- row_clip: int32 [4096], P('tiles'), may hold values from 0 to 7, as said below
- residual: bfloat16 [4096, 3072], P('tiles'), may hold values from -3 to 3
- gate: float32 [8, 3072], replicated, may hold values from 0.5 to 2.5
- out_weight: bfloat16 [1536, 3072], replicated, may hold values from -0.15625 to 0.15625
Outputs:
- block_output: bfloat16 [4096, 3072], P('tiles')
Inputs may be any that keep to these rules, and one draw needn't show every extreme that they name: `destination`: a permutation of the 4096 tile positions; position p is held by device p // 128; the rows of one device send at most 8 rows to one device, and some pair reaches 8 in every draw. `row_clip`: in tile order (row r at position destination[r]) every clip takes one contiguous run of positions, clips numbered in increasing order.
All inputs are finite; a program needn't handle non-finite values.
Results may differ from a plain program's by a relative error of at most 0.0027.
Values may be sent and summed in bfloat16 or wider, within the bound.
A program may use at most 64 MiB of HBM per device.

v0:
```python
import math

import jax
import jax.numpy as jnp
from jax import lax
from jax.sharding import PartitionSpec as P

HEAD_DIM = 128


def as_sent(array):
    return jax.tree.map(lambda a: a.astype(jnp.bfloat16) if a.dtype == jnp.float32 else a, array)


def from_partner(block, axis, bit):
    count = lax.axis_size(axis)
    route = []
    for low in range(count):
        high = low | 1 << bit
        if high != low and high < count:
            route += [(low, high), (high, low)]
    return lax.ppermute(block, axis, route)


def attend_heads(tile_queries, tile_keys, tile_values, query_clip, key_clip):
    head_count = tile_queries.shape[1] // HEAD_DIM
    softmax_scale = 1.0 / math.sqrt(HEAD_DIM)
    same_clip = query_clip[:, None] == key_clip[None, :]

    def one_head(operands):
        query_head, key_head, value_head = operands
        scores = (
            lax.dot_general(
                query_head, key_head, (((1,), (1,)), ((), ())), preferred_element_type=jnp.float32
            )
            * softmax_scale
        )
        scores = jnp.where(same_clip, scores, -1e30)
        row_max = jnp.max(scores, axis=1, keepdims=True)
        weights = jnp.exp(scores - row_max)
        denominator = jnp.sum(weights, axis=1, keepdims=True)
        probabilities = weights.astype(jnp.bfloat16)
        mixture = (
            jnp.dot(probabilities, value_head, preferred_element_type=jnp.float32) / denominator
        )
        return mixture.astype(jnp.bfloat16)

    def split_heads(matrix):
        return matrix.reshape(matrix.shape[0], head_count, HEAD_DIM).transpose(1, 0, 2)

    attended = lax.map(
        one_head, (split_heads(tile_queries), split_heads(tile_keys), split_heads(tile_values))
    )
    return attended.transpose(1, 0, 2).reshape(tile_queries.shape[0], -1)


def finish(attended, residual, query_clip, gate, out_weight):
    projected = jnp.dot(attended, out_weight, preferred_element_type=jnp.float32)
    lookup = (query_clip[:, None] == jnp.arange(gate.shape[0], dtype=jnp.int32)[None, :]).astype(
        jnp.float32
    )
    gate_rows = jnp.dot(lookup, gate, precision=lax.Precision.HIGHEST)
    return (residual.astype(jnp.float32) + gate_rows * projected).astype(jnp.bfloat16)


def rank_within(bucket, bucket_count):
    one_hot = (bucket[:, None] == jnp.arange(bucket_count, dtype=jnp.int32)[None, :]).astype(
        jnp.int32
    )
    running = jnp.cumsum(one_hot, axis=0)
    return jnp.take_along_axis(running, bucket[:, None], axis=1)[:, 0] - 1


def fill_slots(source_rows, position, slot_total, blank):
    return (
        jnp.full((slot_total,) + source_rows.shape[1:], blank, source_rows.dtype)
        .at[position]
        .set(source_rows)
    )


def place_rows(arrived, placement, row_total):
    return (
        jnp.zeros((row_total,) + arrived.shape[1:], arrived.dtype)
        .at[placement]
        .set(arrived, mode="drop")
    )


def shards(queries, keys, values, destination, row_clip, residual, gate, out_weight):
    tile_rows = queries.shape[0]
    peer_count = lax.axis_size("tiles")
    capacity = 2 * tile_rows // peer_count
    target = destination // tile_rows
    slot_index = destination % tile_rows
    slot_total = peer_count * capacity
    position = target * capacity + rank_within(target, peer_count)
    got_queries, got_keys, got_values, got_slots, got_clips = (
        lax.all_to_all(
            fill_slots(queries, position, slot_total, 0),
            "tiles",
            split_axis=0,
            concat_axis=0,
            tiled=True,
        ),
        lax.all_to_all(
            fill_slots(keys, position, slot_total, 0),
            "tiles",
            split_axis=0,
            concat_axis=0,
            tiled=True,
        ),
        lax.all_to_all(
            fill_slots(values, position, slot_total, 0),
            "tiles",
            split_axis=0,
            concat_axis=0,
            tiled=True,
        ),
        lax.all_to_all(
            fill_slots(slot_index, position, slot_total, -1),
            "tiles",
            split_axis=0,
            concat_axis=0,
            tiled=True,
        ),
        lax.all_to_all(
            fill_slots(row_clip, position, slot_total, 0),
            "tiles",
            split_axis=0,
            concat_axis=0,
            tiled=True,
        ),
    )
    placement = jnp.where(got_slots >= 0, got_slots, tile_rows)
    local_queries = place_rows(got_queries, placement, tile_rows)
    local_keys = place_rows(got_keys, placement, tile_rows)
    local_values = place_rows(got_values, placement, tile_rows)
    query_clip = place_rows(got_clips, placement, tile_rows)
    near_keys, near_values, near_clips = (
        from_partner(local_keys, "tiles", 0),
        from_partner(local_values, "tiles", 0),
        from_partner(as_sent(query_clip), "tiles", 0).astype(query_clip.dtype),
    )
    pair_keys = jnp.concatenate([local_keys, near_keys], axis=0)
    pair_values = jnp.concatenate([local_values, near_values], axis=0)
    pair_clips = jnp.concatenate([query_clip, near_clips], axis=0)
    far_keys, far_values, far_clips = (
        from_partner(pair_keys, "tiles", 1),
        from_partner(pair_values, "tiles", 1),
        from_partner(as_sent(pair_clips), "tiles", 1).astype(pair_clips.dtype),
    )
    window_keys = jnp.concatenate([pair_keys, far_keys], axis=0)
    window_values = jnp.concatenate([pair_values, far_values], axis=0)
    key_clip = jnp.concatenate([pair_clips, far_clips], axis=0)
    attended = attend_heads(local_queries, window_keys, window_values, query_clip, key_clip)
    return finish(attended, residual, query_clip, gate, out_weight)


def solution(mesh):
    in_specs = (
        P("tiles", None),
        P("tiles", None),
        P("tiles", None),
        P("tiles"),
        P("tiles"),
        P("tiles", None),
        P(),
        P(),
    )
    out_specs = P("tiles", None)
    return jax.shard_map(shards, mesh=mesh, in_specs=in_specs, out_specs=out_specs, check_vma=False)
```

profile of v0, /device:TPU:13, one launch (start us, length us, event | category | flops | bytes accessed | tf_op | source)
XLA Modules:
  0.0 176.1 jit_solution(8106397041430238353)
XLA Ops:
  1.0 1.3 gather_fusion
  4.0 6.3 %all-to-all-start = ((s32[32,8,1]{1,2,0:T(1,128)}), s32[32,8,1]{1,2,0:T(1,128)S(1)}, u32[]{:S(2)}, u32[]{:S(2)}) async-start(s32[32,8,1]{1,2,0:T(1,128)} %bitcast.3), calls=%async_computation | async-start | bytes 32768 | tf_op jit(solution)/shard_map/all_to_all | solution.py:120
  12.1 2.8 %all-to-all-done = s32[32,8,1]{1,2,0:T(1,128)S(1)} async-done(((s32[32,8,1]{1,2,0:T(1,128)}), s32[32,8,1]{1,2,0:T(1,128)S(1)}, u32[]{:S(2)}, u32[]{:S(2)}) %all-to-all-start) | async-done | bytes 1056 | tf_op jit(solution)/shard_map/all_to_all | solution.py:120
  14.9 4.9 %all-to-all-start.1 = ((s32[32,8,1]{1,2,0:T(1,128)}), s32[32,8,1]{1,2,0:T(1,128)S(1)}, u32[]{:S(2)}, u32[]{:S(2)}) async-start(s32[32,8,1]{1,2,0:T(1,128)} %bitcast.5), calls=%async_computation.1 | async-start | bytes 32768 | tf_op jit(solution)/shard_map/all_to_all | solution.py:127
  19.9 2.6 %scatter_custom_fusion.7 = bf16[256,1536]{1,0:T(8,128)(2,1)} fusion(s32[128]{0:T(128)S(1)} %compare_select_fusion.2, bf16[128,1536]{1,0:T(8,128)(2,1)} %param.12, bf16[]{:T(256)} %constant.80.clone.1), kind=kCustom, calls=%fused_computation.42 | custom fusion | bytes 786944 | tf_op jit(solution)/shard_map/scatter | solution.py:78
  22.5 2.2 %all-to-all-done.1 = s32[32,8,1]{1,2,0:T(1,128)S(1)} async-done(((s32[32,8,1]{1,2,0:T(1,128)}), s32[32,8,1]{1,2,0:T(1,128)S(1)}, u32[]{:S(2)}, u32[]{:S(2)}) %all-to-all-start.1) | async-done | bytes 1056 | tf_op jit(solution)/shard_map/all_to_all | solution.py:127
  24.7 5.0 %all-to-all-start.4 = ((bf16[32,8,1536]{2,1,0:T(8,128)(2,1)}), bf16[32,8,1536]{2,1,0:T(8,128)(2,1)S(1)}, u32[]{:S(2)}, u32[]{:S(2)}) async-start(bf16[32,8,1536]{2,1,0:T(8,128)(2,1)} %bitcast.14), calls=%async_computation.4 | async-start | bytes 1572864 | tf_op jit(solution)/shard_map/all_to_all | solution.py:113
  29.7 2.6 %scatter_custom_fusion.5 = bf16[256,1536]{1,0:T(8,128)(2,1)} fusion(s32[128]{0:T(128)S(1)} %compare_select_fusion.2, bf16[128,1536]{1,0:T(8,128)(2,1)} %param.11, bf16[]{:T(256)} %constant.80.clone.1), kind=kCustom, calls=%fused_computation.44 | custom fusion | bytes 786944 | tf_op jit(solution)/shard_map/scatter | solution.py:78
  32.3 15.9 %all-to-all-done.4 = bf16[32,8,1536]{2,1,0:T(8,128)(2,1)S(1)} async-done(((bf16[32,8,1536]{2,1,0:T(8,128)(2,1)}), bf16[32,8,1536]{2,1,0:T(8,128)(2,1)S(1)}, u32[]{:S(2)}, u32[]{:S(2)}) %all-to-all-start.4) | async-done | bytes 786464 | tf_op jit(solution)/shard_map/all_to_all | solution.py:113
  48.2 5.7 %all-to-all-start.3 = ((bf16[32,8,1536]{2,1,0:T(8,128)(2,1)}), bf16[32,8,1536]{2,1,0:T(8,128)(2,1)S(1)}, u32[]{:S(2)}, u32[]{:S(2)}) async-start(bf16[32,8,1536]{2,1,0:T(8,128)(2,1)} %bitcast.10), calls=%async_computation.3 | async-start | bytes 1572864 | tf_op jit(solution)/shard_map/all_to_all | solution.py:106
  53.9 2.6 %scatter_custom_fusion.3 = bf16[256,1536]{1,0:T(8,128)(2,1)} fusion(s32[128]{0:T(128)S(1)} %compare_select_fusion.2, bf16[128,1536]{1,0:T(8,128)(2,1)} %param.10, bf16[]{:T(256)} %constant.80.clone.1), kind=kCustom, calls=%fused_computation.46 | custom fusion | bytes 786944 | tf_op jit(solution)/shard_map/scatter | solution.py:78
  57.8 14.5 %all-to-all-done.3 = bf16[32,8,1536]{2,1,0:T(8,128)(2,1)S(1)} async-done(((bf16[32,8,1536]{2,1,0:T(8,128)(2,1)}), bf16[32,8,1536]{2,1,0:T(8,128)(2,1)S(1)}, u32[]{:S(2)}, u32[]{:S(2)}) %all-to-all-start.3) | async-done | bytes 786464 | tf_op jit(solution)/shard_map/all_to_all | solution.py:106
  72.3 5.8 %all-to-all-start.2 = ((bf16[32,8,1536]{2,1,0:T(8,128)(2,1)}), bf16[32,8,1536]{2,1,0:T(8,128)(2,1)S(1)}, u32[]{:S(2)}, u32[]{:S(2)}) async-start(bf16[32,8,1536]{2,1,0:T(8,128)(2,1)} %bitcast.6), calls=%async_computation.2 | async-start | bytes 1572864 | tf_op jit(solution)/shard_map/all_to_all | solution.py:99
  78.1 1.9 %scatter_custom_fusion.8 = bf16[128,1536]{1,0:T(8,128)(2,1)S(1)} fusion(s32[256]{0:T(256)S(1)} %bitcast.68, bf16[32,8,1536]{2,1,0:T(8,128)(2,1)S(1)} %all-to-all-done.4, bf16[]{:T(256)} %constant.80.clone.1), kind=kCustom, calls=%fused_computation.36 | custom fusion | bytes 1179650 | tf_op jit(solution)/shard_map/scatter | solution.py:86
  80.4 1.8 %scatter_custom_fusion.6 = bf16[128,1536]{1,0:T(8,128)(2,1)S(1)} fusion(s32[256]{0:T(256)S(1)} %bitcast.69, bf16[32,8,1536]{2,1,0:T(8,128)(2,1)S(1)} %all-to-all-done.3, bf16[]{:T(256)} %constant.80.clone.1), kind=kCustom, calls=%fused_computation.38 | custom fusion | bytes 1179650 | tf_op jit(solution)/shard_map/scatter | solution.py:86
  82.5 1.2 collective-permute-start.5
  87.7 1.4 scatter_custom_fusion.2
  90.9 32.5 %collective-permute-done.3 = s32[256]{0:T(256)S(1)} collective-permute-done((s32[256]{0:T(256)S(1)}, s32[256]{0:T(256)S(1)}, u32[]{:S(2)}, u32[]{:S(2)}) %collective-permute-start.3) | collective-permute-done | bytes 1056 | tf_op jit(solution)/shard_map/ppermute | solution.py:22
  123.4 2.0 %scatter_custom_fusion.4 = bf16[128,1536]{1,0:T(8,128)(2,1)S(1)} fusion(s32[256]{0:T(256)S(1)} %bitcast.71, bf16[32,8,1536]{2,1,0:T(8,128)(2,1)S(1)} %all-to-all-done.2, bf16[]{:T(256)} %constant.80.clone.1), kind=kCustom, calls=%fused_computation.40 | custom fusion | bytes 1179650 | tf_op jit(solution)/shard_map/scatter | solution.py:86
  126.4 1.3 pad_maximum_fusion.1
  127.7 1.6 copy.27
  131.3 37.6 %while.11 = (s32[]{:T(128)}, bf16[12,128,128]{1,2,0:T(8,128)(2,1)}, bf16[12,128,128]{1,2,0:T(8,128)(2,1)}, bf16[12,512,128]{1,2,0:T(8,128)(2,1)S(1)}, bf16[12,51...) while((s32[]{:T(128)}, bf16[12,128,128]{1,2,0:T(8,128)(2,1)}, ...), condition=%wide.region_13.14_spmd.clone, body=%wide.region_10.13_spmd.clone.sunk | while | flops 34111232 | bytes 1252437 | solution.py:51
  168.9 5.3 %fusion.44 = f32[128,3072]{1,0:T(8,128)S(1)} fusion(bf16[128,1536]{0,1:T(8,128)(2,1)} %bitcast.66, bf16[1536,3072]{1,0:T(8,128)(2,1)} %param.17), kind=kOutput, calls=%fused_computation.77 | convolution fusion | flops 1207959552 | bytes 11403264 | tf_op jit(solution)/shard_map/dot_general | solution.py:58
  174.2 1.8 %fusion.18 = bf16[128,3072]{1,0:T(8,128)(2,1)} fusion(f32[128,3072]{1,0:T(8,128)S(1)} %fusion.44, f32[8,3072]{1,0:T(8,128)S(1)} %copy-done, bf16[128,3072]{1,0:T(8,128)(2,1)S(1)} %copy-done.4, s32[128]{0:T(128)S(1)} %get-tuple-element.178), kind=kOutput, calls=%fused_computation.31 | convolution fusion | flops 39322624 | bytes 3244544 | tf_op jit(solution)/shard_map/dot_general | solution.py:62
  (106 shorter events, 52.5 us)
Async XLA Ops:
  0.0 174.2 %copy-start = (f32[8,3072]{1,0:T(8,128)S(1)}, f32[8,3072]{1,0:T(8,128)}, u32[]{:S(2)}) copy-start(f32[8,3072]{1,0:T(8,128)} %param.16) | copy-start | bytes 294916
  4.0 11.0 %all-to-all-start = ((s32[32,8,1]{1,2,0:T(1,128)}), s32[32,8,1]{1,2,0:T(1,128)S(1)}, u32[]{:S(2)}, u32[]{:S(2)}) async-start(s32[32,8,1]{1,2,0:T(1,128)} %bitcast.3), calls=%async_computation | async-start | bytes 32768 | tf_op jit(solution)/shard_map/all_to_all | solution.py:120
  14.9 9.7 %all-to-all-start.1 = ((s32[32,8,1]{1,2,0:T(1,128)}), s32[32,8,1]{1,2,0:T(1,128)S(1)}, u32[]{:S(2)}, u32[]{:S(2)}) async-start(s32[32,8,1]{1,2,0:T(1,128)} %bitcast.5), calls=%async_computation.1 | async-start | bytes 32768 | tf_op jit(solution)/shard_map/all_to_all | solution.py:127
  24.7 23.5 %all-to-all-start.4 = ((bf16[32,8,1536]{2,1,0:T(8,128)(2,1)}), bf16[32,8,1536]{2,1,0:T(8,128)(2,1)S(1)}, u32[]{:S(2)}, u32[]{:S(2)}) async-start(bf16[32,8,1536]{2,1,0:T(8,128)(2,1)} %bitcast.14), calls=%async_computation.4 | async-start | bytes 1572864 | tf_op jit(solution)/shard_map/all_to_all | solution.py:113
  48.2 24.2 %all-to-all-start.3 = ((bf16[32,8,1536]{2,1,0:T(8,128)(2,1)}), bf16[32,8,1536]{2,1,0:T(8,128)(2,1)S(1)}, u32[]{:S(2)}, u32[]{:S(2)}) async-start(bf16[32,8,1536]{2,1,0:T(8,128)(2,1)} %bitcast.10), calls=%async_computation.3 | async-start | bytes 1572864 | tf_op jit(solution)/shard_map/all_to_all | solution.py:106
  72.3 51.1 %all-to-all-start.2 = ((bf16[32,8,1536]{2,1,0:T(8,128)(2,1)}), bf16[32,8,1536]{2,1,0:T(8,128)(2,1)S(1)}, u32[]{:S(2)}, u32[]{:S(2)}) async-start(bf16[32,8,1536]{2,1,0:T(8,128)(2,1)} %bitcast.6), calls=%async_computation.2 | async-start | bytes 1572864 | tf_op jit(solution)/shard_map/all_to_all | solution.py:99
  80.0 2.5 %collective-permute-start.4 = (bf16[128,1536]{1,0:T(8,128)(2,1)S(1)}, bf16[128,1536]{1,0:T(8,128)(2,1)S(1)}, u32[]{:S(2)}, u32[]{:S(2)}) collective-permute-start(bf16[128,1536]{1,0:T(8,128)(2,1)S(1)} %scatter_custom_fusion.8), channel_id=1, source_target_pairs={{0,1},{1,0},{2,3},{3,2},{4,5},{5,4},{6,7},{7,6},{8,9},{9,8},{10,11... | collective-permute-start | bytes 1179656 | tf_op jit(solution)/shard_map/ppermute | solution.py:22
  82.3 1.8 %collective-permute-start = (bf16[128,1536]{1,0:T(8,128)(2,1)S(1)}, bf16[128,1536]{1,0:T(8,128)(2,1)S(1)}, u32[]{:S(2)}, u32[]{:S(2)}) collective-permute-start(bf16[128,1536]{1,0:T(8,128)(2,1)S(1)} %scatter_custom_fusion.6), channel_id=1, source_target_pairs={{0,1},{1,0},{2,3},{3,2},{4,5},{5,4},{6,7},{7,6},{8,9},{9,8},{10,11... | collective-permute-start | bytes 1179656 | tf_op jit(solution)/shard_map/ppermute | solution.py:22
  82.5 3.3 %copy-start.3 = (bf16[128,1536]{1,0:T(8,128)(2,1)}, bf16[128,1536]{1,0:T(8,128)(2,1)S(1)}, u32[]{:S(2)}) copy-start(bf16[128,1536]{1,0:T(8,128)(2,1)S(1)} %collective-permute-done.4) | copy-start | bytes 1179652
  82.5 43.8 %collective-permute-start.5 = (bf16[256,1536]{1,0:T(8,128)(2,1)S(1)}, bf16[256,1536]{1,0:T(8,128)(2,1)}, u32[]{:S(2)}, u32[]{:S(2)}) collective-permute-start(bf16[256,1536]{1,0:T(8,128)(2,1)S(1)} %pad_maximum_fusion.3), channel_id=1, source_target_pairs={{0,2},{2,0},{1,3},{3,1},{4,6},{6,4},{5,7},{7,5},{8,10},{10,8},{9,1... | collective-permute-start | bytes 2359304 | tf_op jit(solution)/shard_map/ppermute | solution.py:22
  84.1 0.7 copy-start.1
  85.7 43.6 %collective-permute-start.1 = (bf16[256,1536]{1,0:T(8,128)(2,1)}, bf16[256,1536]{1,0:T(8,128)(2,1)}, u32[]{:S(2)}, u32[]{:S(2)}) collective-permute-start(bf16[256,1536]{1,0:T(8,128)(2,1)} %pad_maximum_fusion.2), channel_id=1, source_target_pairs={{0,2},{2,0},{1,3},{3,1},{4,6},{6,4},{5,7},{7,5},{8,10},{10,8},{9,1... | collective-permute-start | bytes 2359304 | tf_op jit(solution)/shard_map/ppermute | solution.py:22
  89.1 1.3 collective-permute-start.2
  90.4 33.0 %collective-permute-start.3 = (s32[256]{0:T(256)S(1)}, s32[256]{0:T(256)S(1)}, u32[]{:S(2)}, u32[]{:S(2)}) collective-permute-start(s32[256]{0:T(256)S(1)} %pad_add_fusion.1), channel_id=1, source_target_pairs={{0,2},{2,0},{1,3},{3,1},{4,6},{6,4},{5,7},{7,5},{8,10},{10,8},{9,1... | collective-permute-start | bytes 3080 | tf_op jit(solution)/shard_map/ppermute | solution.py:22
  127.7 1.6 copy-start.2
  168.9 5.3 %copy-start.4 = (bf16[128,3072]{1,0:T(8,128)(2,1)S(1)}, bf16[128,3072]{1,0:T(8,128)(2,1)}, u32[]{:S(2)}) copy-start(bf16[128,3072]{1,0:T(8,128)(2,1)} %param.15) | copy-start | bytes 2359300
where the time goes:
time: 179 us; the launch traced here: 176 us
  waiting for transfers between devices  69 us (39%)
  matrix products  33.5 us (19%)
  local copies, waits for them, and re-layouts  33.2 us (19%)
  starting transfers between devices  31.8 us (18%)
  other arithmetic  8.25 us (5%)
    ppermute x6, waiting for transfers between devices, from_partner(): return lax.ppermute(block, axis, route)  33.5 us
    all_to_all x1, waiting for transfers between devices, shards(): lax.all_to_all(fill_slots(values, position, slot_total, 0), 'tiles', spli...  15.9 us
    all_to_all x1, waiting for transfers between devices, shards(): lax.all_to_all(fill_slots(keys, position, slot_total, 0), 'tiles', split_...  14.5 us
    dot_general x12, matrix products, one_head(): jnp.dot(probabilities, value_head, preferred_element_type=jnp.float32)  13.8 us
    dot_general x12, matrix products, one_head(): lax.dot_general(query_head, key_head, (((1,), (1,)), ((), ())), preferred...  12.6 us
    scatter x5, local copies, waits for them, and re-layouts, fill_slots(): return jnp.full((slot_total,) + source_rows.shape[1:], blank, source_rows...  9.92 us
    dynamic_update_slice x24, local copies, waits for them, and re-layouts, attend_heads(): lax.map(one_head, (split_heads(tile_queries), split_heads(tile_keys), spl...  8.73 us
    scatter x5, local copies, waits for them, and re-layouts, place_rows(): return jnp.zeros((row_total,) + arrived.shape[1:], arrived.dtype).at[plac...  8.05 us
  transfers between devices with their start and end apart: 11, of which 7 were waited for; matrix products, arithmetic and copies ran while one was open for 13% of the time, Pallas kernels for 0%

commit v1 on v0

v1 whole, which is shorter than its diff:
```python
import functools
import math

import jax
import jax.numpy as jnp
from jax import lax
from jax.experimental import pallas as pl
from jax.experimental.pallas import tpu as pltpu
from jax.sharding import PartitionSpec as P

HEAD_DIM = 128
GROUP = 4
MESH = pl.DeviceIdType.MESH
F32 = jnp.float32
BF16 = jnp.bfloat16


def kernel(
    n,
    slots,
    q_ref,
    k_ref,
    v_ref,
    dest_ref,
    clip_ref,
    gate_ref,
    residual_hbm,
    weight_hbm,
    out_ref,
    send,
    recv,
    meta_send,
    meta_recv,
    pick,
    clip_col,
    bias,
    att_send,
    att,
    total,
    gate_rows,
    weight,
    residual,
    send_sem,
    recv_sem,
    meta_send_sem,
    meta_recv_sem,
    back_send_sem,
    back_recv_sem,
    load_sem,
    own_sem,
):
    tile = q_ref.shape[0]
    chunks = q_ref.shape[1] // (GROUP * HEAD_DIM)
    wide = GROUP * HEAD_DIM
    window = GROUP * tile
    windows = n // GROUP
    me = lax.axis_index("tiles")
    my_window = me // GROUP
    mine = me % GROUP

    barrier = pltpu.get_barrier_semaphore()

    def greet(o, carry):
        pl.semaphore_signal(barrier, inc=1, device_id=((me + o) % n,), device_id_type=MESH)
        return carry

    lax.fori_loop(1, n, greet, 0)

    load_weight = pltpu.make_async_copy(weight_hbm, weight, load_sem.at[0])
    load_residual = pltpu.make_async_copy(residual_hbm, residual, load_sem.at[1])

    dest_row = dest_ref[...]
    win_row = lax.div(dest_row, jnp.int32(window))
    code_row = lax.rem(dest_row, jnp.int32(window)) + 1 + clip_ref[...] * 1024
    line = lax.broadcasted_iota(jnp.int32, (tile, tile), 0)
    lane = lax.broadcasted_iota(jnp.int32, (tile, tile), 1)
    eye = line == lane

    def to_column(row):
        wide_row = jnp.broadcast_to(row.astype(F32), (tile, tile))
        return jnp.sum(jnp.where(eye, wide_row, 0.0), axis=1, keepdims=True).astype(jnp.int32)

    win_col = to_column(win_row)
    code_col = to_column(code_row)
    same = win_col == win_row
    rank_row = jnp.sum(jnp.where(same & (line < lane), 1.0, 0.0), axis=0, keepdims=True)
    rank_col = jnp.sum(jnp.where(same & (lane < line), 1.0, 0.0), axis=1, keepdims=True)
    slot_row = win_row * slots + rank_row.astype(jnp.int32)
    slot_col = win_col * 128 + rank_col.astype(jnp.int32)

    spread = lax.broadcasted_iota(jnp.int32, (tile, 128), 1) % slots
    for w in range(windows):
        hit = slot_col == spread + w * 128
        codes = jnp.sum(jnp.where(hit, code_col.astype(F32), 0.0), axis=0, keepdims=True)
        meta_send[w] = codes.astype(jnp.int32)

    slot_line = lax.broadcasted_iota(jnp.int32, (windows * slots, tile), 0)
    place = jnp.where(slot_line == slot_row, 1.0, 0.0).astype(BF16)

    def order(i):
        return n // 2 + (1 - 2 * (i % 2)) * ((i + 1) // 2)

    def meta_copy(o):
        to = (me + o) % n
        return pltpu.make_async_remote_copy(
            src_ref=meta_send.at[to // GROUP],
            dst_ref=meta_recv.at[me],
            send_sem=meta_send_sem.at[o],
            recv_sem=meta_recv_sem.at[me],
            device_id=(to,),
            device_id_type=MESH,
        )

    def meta_arrival(o):
        come = (me + o) % n
        return pltpu.make_async_remote_copy(
            src_ref=meta_send.at[0],
            dst_ref=meta_recv.at[come],
            send_sem=meta_send_sem.at[o],
            recv_sem=meta_recv_sem.at[come],
            device_id=(come,),
            device_id_type=MESH,
        )

    def copy(c, o):
        to = (me + o) % n
        return pltpu.make_async_remote_copy(
            src_ref=send.at[c, to // GROUP, to % GROUP],
            dst_ref=recv.at[c, me],
            send_sem=send_sem.at[c, o],
            recv_sem=recv_sem.at[c, me],
            device_id=(to,),
            device_id_type=MESH,
        )

    def arrival(c, o):
        come = (me + o) % n
        return pltpu.make_async_remote_copy(
            src_ref=send.at[c, 0, 0],
            dst_ref=recv.at[c, come],
            send_sem=send_sem.at[c, o],
            recv_sem=recv_sem.at[c, come],
            device_id=(come,),
            device_id_type=MESH,
        )

    def own_copy(c):
        return pltpu.make_async_copy(
            send.at[c, my_window, mine], recv.at[c, me], own_sem.at[c]
        )

    own_meta = pltpu.make_async_copy(meta_send.at[my_window], meta_recv.at[me], own_sem.at[chunks])

    for c in range(chunks):
        for t, ref in enumerate((q_ref, k_ref, v_ref)):
            packed = jnp.dot(
                place, ref[:, c * wide : (c + 1) * wide], preferred_element_type=F32
            ).astype(BF16)
            for j in range(GROUP):
                part = packed[:, j * HEAD_DIM : (j + 1) * HEAD_DIM]
                send[c, :, j, :, t * HEAD_DIM : (t + 1) * HEAD_DIM] = part.reshape(
                    windows, slots, HEAD_DIM
                )
        if c == 0:
            pl.semaphore_wait(barrier, n - 1)

            def start_meta(i, carry):
                meta_copy(order(i)).start()
                return carry

            lax.fori_loop(0, n - 1, start_meta, 0)
            own_meta.start()

        def start_chunk(i, carry, c=c):
            copy(c, order(i)).start()
            return carry

        lax.fori_loop(0, n - 1, start_chunk, 0)
        own_copy(c).start()

    load_weight.start()
    load_residual.start()

    def wait_meta(o, carry):
        meta_arrival(o).wait_recv()
        return carry

    lax.fori_loop(1, n, wait_meta, 0)
    own_meta.wait()
    per_row = 128 // slots
    lane_block = lax.broadcasted_iota(jnp.int32, (1, 128), 1) // slots
    rows = []
    for g in range(n // per_row):
        row = jnp.zeros((1, 128), jnp.int32)
        for i in range(per_row):
            row = jnp.where(lane_block == i, meta_recv[g * per_row + i], row)
        rows.append(row)
    for b in range(GROUP):
        spot = lax.broadcasted_iota(jnp.int32, (tile, 128), 0) + (b * tile + 1)
        sums = jnp.zeros((tile, 128), F32)
        for g, row in enumerate(rows):
            hit = spot == (row & 1023)
            pick[b * tile : (b + 1) * tile, g * 128 : (g + 1) * 128] = jnp.where(
                hit, 1.0, 0.0
            ).astype(BF16)
            sums = sums + jnp.where(hit, (row >> 10).astype(F32), 0.0)
        column = jnp.sum(sums, axis=1, keepdims=True)
        clip_col[b * tile : (b + 1) * tile, :] = jnp.broadcast_to(column, (tile, 128))
    for b in range(GROUP):
        key_clip = jnp.sum(
            jnp.where(eye, clip_col[b * tile : (b + 1) * tile, :], 0.0), axis=0, keepdims=True
        )
        for a in range(GROUP):
            query_clip = clip_col[a * tile : (a + 1) * tile, :]
            bias[a * tile : (a + 1) * tile, b * tile : (b + 1) * tile] = jnp.where(
                query_clip == key_clip, 0.0, -1e30
            )

    clips = gate_ref.shape[0]
    my_clip = clip_col[pl.ds(pl.multiple_of(mine * tile, tile), tile), :]
    lookup = jnp.where(
        my_clip[:, :clips] == lax.broadcasted_iota(jnp.int32, (tile, clips), 1).astype(F32), 1.0, 0.0
    )
    width = out_ref.shape[1]
    for x in range(0, width, 512):
        gate_rows[:, x : x + 512] = jnp.dot(
            lookup,
            gate_ref[:, x : x + 512],
            precision=lax.Precision.HIGHEST,
            preferred_element_type=F32,
        )
    load_weight.wait()
    load_residual.wait()

    def back_copy(c, o):
        to = (mine + o) % GROUP
        return pltpu.make_async_remote_copy(
            src_ref=att_send.at[c, to],
            dst_ref=att.at[c, mine],
            send_sem=back_send_sem.at[c, o],
            recv_sem=back_recv_sem.at[c, mine],
            device_id=(my_window * GROUP + to,),
            device_id_type=MESH,
        )

    def back_arrival(c, o):
        come = (mine + o) % GROUP
        return pltpu.make_async_remote_copy(
            src_ref=att_send.at[c, 0],
            dst_ref=att.at[c, come],
            send_sem=back_send_sem.at[c, o],
            recv_sem=back_recv_sem.at[c, come],
            device_id=(my_window * GROUP + come,),
            device_id_type=MESH,
        )

    def project(c):
        for o in range(1, GROUP):
            back_arrival(c, o).wait_recv()
        own_back(c).wait()
        attended = jnp.concatenate([att[c, j] for j in range(GROUP)], axis=1)
        for x in range(0, width, 512):
            part = jnp.dot(
                attended,
                weight[c * wide : (c + 1) * wide, x : x + 512],
                preferred_element_type=F32,
            )
            if c > 0:
                part = part + total[:, x : x + 512]
            if c < chunks - 1:
                total[:, x : x + 512] = part
            else:
                out_ref[:, x : x + 512] = (
                    residual[:, x : x + 512].astype(F32) + gate_rows[:, x : x + 512] * part
                ).astype(out_ref.dtype)

    def own_back(c):
        return pltpu.make_async_copy(
            att_send.at[c, mine], att.at[c, mine], own_sem.at[chunks + 1 + c]
        )

    scale = 1.0 / math.sqrt(HEAD_DIM)
    for c in range(chunks):

        def wait_chunk(o, carry, c=c):
            arrival(c, o).wait_recv()
            return carry

        lax.fori_loop(1, n, wait_chunk, 0)
        own_copy(c).wait()
        arrived = recv[c].reshape(n * slots, 3 * HEAD_DIM)
        rows_qkv = jnp.dot(pick[...], arrived, preferred_element_type=F32).astype(BF16)
        keys = rows_qkv[:, HEAD_DIM : 2 * HEAD_DIM]
        vals = rows_qkv[:, 2 * HEAD_DIM :]
        for b in range(GROUP):
            queries = rows_qkv[b * tile : (b + 1) * tile, :HEAD_DIM]
            scores = (
                lax.dot_general(
                    queries, keys, (((1,), (1,)), ((), ())), preferred_element_type=F32
                )
                * scale
                + bias[b * tile : (b + 1) * tile, :]
            )
            top = jnp.max(scores, axis=1, keepdims=True)
            weights = jnp.exp(scores - top)
            denominator = jnp.sum(weights, axis=1, keepdims=True)
            mixture = jnp.dot(weights.astype(BF16), vals, preferred_element_type=F32)
            att_send[c, b] = (mixture / denominator).astype(BF16)
        for o in range(1, GROUP):
            back_copy(c, o).start()
        own_back(c).start()
        if c > 0:
            project(c - 1)
    project(chunks - 1)

    def wait_sent(o, carry):
        meta_copy(o).wait_send()
        for c in range(chunks):
            copy(c, o).wait_send()
        return carry

    lax.fori_loop(1, n, wait_sent, 0)
    for c in range(chunks):
        for o in range(1, GROUP):
            back_copy(c, o).wait_send()


def shards(queries, keys, values, destination, row_clip, residual, gate, out_weight):
    n = lax.axis_size("tiles")
    tile, features = queries.shape
    width = residual.shape[1]
    chunks = features // (GROUP * HEAD_DIM)
    windows = n // GROUP
    slots = max(GROUP * (2 * tile // n), 16)
    window = GROUP * tile
    vmem = pl.BlockSpec(memory_space=pltpu.VMEM)
    anywhere = pl.BlockSpec(memory_space=pl.ANY)
    dma = pltpu.SemaphoreType.DMA
    return pl.pallas_call(
        functools.partial(kernel, n, slots),
        out_shape=jax.ShapeDtypeStruct((tile, width), BF16),
        in_specs=[vmem] * 6 + [anywhere] * 2,
        out_specs=vmem,
        scratch_shapes=[
            pltpu.VMEM((chunks, windows, GROUP, slots, 3 * HEAD_DIM), BF16),
            pltpu.VMEM((chunks, n, slots, 3 * HEAD_DIM), BF16),
            pltpu.VMEM((windows, 1, 128), jnp.int32),
            pltpu.VMEM((n, 1, 128), jnp.int32),
            pltpu.VMEM((window, n * slots), BF16),
            pltpu.VMEM((window, 128), F32),
            pltpu.VMEM((window, window), F32),
            pltpu.VMEM((chunks, GROUP, tile, HEAD_DIM), BF16),
            pltpu.VMEM((chunks, GROUP, tile, HEAD_DIM), BF16),
            pltpu.VMEM((tile, width), F32),
            pltpu.VMEM((tile, width), F32),
            pltpu.VMEM((features, width), BF16),
            pltpu.VMEM((tile, width), BF16),
            dma((chunks, n)),
            dma((chunks, n)),
            dma((n,)),
            dma((n,)),
            dma((chunks, GROUP)),
            dma((chunks, GROUP)),
            dma((2,)),
            dma((2 * chunks + 1,)),
        ],
        compiler_params=pltpu.CompilerParams(
            collective_id=0, has_side_effects=True, vmem_limit_bytes=50 * 1024 * 1024
        ),
    )(
        queries,
        keys,
        values,
        destination.reshape(1, tile),
        row_clip.reshape(1, tile),
        gate,
        residual,
        out_weight,
    )


def solution(mesh):
    rows = P("tiles", None)
    in_specs = (rows, rows, rows, P("tiles"), P("tiles"), rows, P(), P())
    return jax.shard_map(shards, mesh=mesh, in_specs=in_specs, out_specs=rows, check_vma=False)
```

time: 179 us -> 74 us (0.41); the launches traced: 176 us -> 73.7 us
  waiting for transfers between devices: 69 us -> 0 us
  Pallas kernels: 0 us -> 66.5 us
  matrix products: 33.5 us -> 0 us
  starting transfers between devices: 31.8 us -> 0 us
  local copies, waits for them, and re-layouts: 33.2 us -> 7.2 us
  other arithmetic: 8.25 us -> 0 us
    pallas_call x0 -> x1, Pallas kernels: none -> 66.5 us  [shards(): pl.pallas_call(functools.partial(kernel, n, slots), out_shape=jax.ShapeDt...]
    all_to_all x5 -> x0, waiting for transfers between devices: 35.4 us -> none  [the longest x1 15.9 us: shards(): lax.all_to_all(fill_slots(values, position, slot_total, 0), 'tiles', spli...]
    ppermute x6 -> x0, waiting for transfers between devices: 33.5 us -> none  [from_partner(): return lax.ppermute(block, axis, route)]
    dot_general x26 -> x0, matrix products: 33.5 us -> none  [the longest x12 13.8 us: one_head(): jnp.dot(probabilities, value_head, preferred_element_type=jnp.float32)]
    all_to_all x5 -> x0, starting transfers between devices: 27.7 us -> none  [the longest x1 6.3 us: shards(): lax.all_to_all(fill_slots(slot_index, position, slot_total, -1), 'tiles',...]
    scatter x10 -> x0, local copies, waits for them, and re-layouts: 18 us -> none  [the longest x5 9.92 us: fill_slots(): return jnp.full((slot_total,) + source_rows.shape[1:], blank, source_rows...]
    dynamic_update_slice x24 -> x0, local copies, waits for them, and re-layouts: 8.73 us -> none  [attend_heads(): lax.map(one_head, (split_heads(tile_queries), split_heads(tile_keys), spl...]
    unnamed x11 -> x15, local copies, waits for them, and re-layouts: 0.76 us -> 7.2 us
  transfers between devices with their start and end apart: 11 -> 0, of which waited for: 7 -> 0; matrix products, arithmetic and copies ran while one was open for 13% -> 0% of each run, Pallas kernels for 0% -> 0%
where the time goes in v1:
time: 74 us; the launch traced here: 73.7 us
  Pallas kernels  66.5 us (90%)
  local copies, waits for them, and re-layouts  7.2 us (10%)
    pallas_call x1, Pallas kernels, shards(): pl.pallas_call(functools.partial(kernel, n, slots), out_shape=jax.ShapeDt...  66.5 us
    unnamed x15, local copies, waits for them, and re-layouts  7.2 us

profile of v1, /device:TPU:13, one launch (start us, length us, event | category | flops | bytes accessed | tf_op | source)
XLA Modules:
  0.0 73.7 jit_solution(881089106225447682)
XLA Ops:
  0.0 0.0 copy-start
  0.0 1.1 %copy-done = bf16[128,3072]{1,0:T(8,128)(2,1)S(1)} copy-done((bf16[128,3072]{1,0:T(8,128)(2,1)S(1)}, bf16[128,3072]{1,0:T(8,128)(2,1)}, u32[]{:S(2)}) %copy-start) | copy-done | bytes 786456
  1.1 0.0 copy-start.1
  1.1 1.0 %copy-done.1 = bf16[128,1536]{1,0:T(8,128)(2,1)S(1)} copy-done((bf16[128,1536]{1,0:T(8,128)(2,1)S(1)}, bf16[128,1536]{1,0:T(8,128)(2,1)}, u32[]{:S(2)}) %copy-start.1) | copy-done | bytes 393240
  2.1 0.0 copy-start.2
  2.1 1.0 %copy-done.2 = bf16[128,1536]{1,0:T(8,128)(2,1)S(1)} copy-done((bf16[128,1536]{1,0:T(8,128)(2,1)S(1)}, bf16[128,1536]{1,0:T(8,128)(2,1)}, u32[]{:S(2)}) %copy-start.2) | copy-done | bytes 393240
  3.1 0.0 copy-start.3
  3.1 1.0 %copy-done.3 = bf16[128,1536]{1,0:T(8,128)(2,1)S(1)} copy-done((bf16[128,1536]{1,0:T(8,128)(2,1)S(1)}, bf16[128,1536]{1,0:T(8,128)(2,1)}, u32[]{:S(2)}) %copy-start.3) | copy-done | bytes 393240
  4.1 0.0 copy-start.4
  4.1 0.9 %copy-done.4 = f32[8,3072]{1,0:T(8,128)S(1)} copy-done((f32[8,3072]{1,0:T(8,128)S(1)}, f32[8,3072]{1,0:T(8,128)}, u32[]{:S(2)}) %copy-start.4) | copy-done | bytes 98328
  5.0 0.0 copy-start.5
  5.0 0.7 copy-done.5
  5.7 0.0 copy-start.6
  5.7 0.7 copy-done.6
  6.3 66.5 %shard_map.82 = bf16[128,3072]{1,0:T(8,128)(2,1)S(1)} custom-call(bf16[128,1536]{1,0:T(8,128)(2,1)S(1)} %copy-done.1, bf16[128,1536]{1,0:T(8,128)(2,1)S(1)} %copy-done.2, bf16[128,1536]{1,0:T(8,128)(2,1)S(1)} %copy-done.3, s32[1,128]{1,0:T(1,128)S(1)} %bitcast.2, s32[1,128]{1,0:T(1,128)S(1)} %bitcast.3, f32[8,3072]{1,0:T(8,128)S(1)} %copy-done.4, ...), custom_call_target="tpu_custom_call" | custom-call | tf_op jit(solution)/shard_map/pallas_call | solution.py:339
  72.8 0.9 %copy.10 = bf16[128,3072]{1,0:T(8,128)(2,1)} copy(bf16[128,3072]{1,0:T(8,128)(2,1)S(1)} %shard_map.82) | data formatting | bytes 1572864
Async XLA Ops:
  0.0 1.1 %copy-start = (bf16[128,3072]{1,0:T(8,128)(2,1)S(1)}, bf16[128,3072]{1,0:T(8,128)(2,1)}, u32[]{:S(2)}) copy-start(bf16[128,3072]{1,0:T(8,128)(2,1)} %residual_hbm.1) | copy-start | bytes 2359300
  1.1 1.0 %copy-start.1 = (bf16[128,1536]{1,0:T(8,128)(2,1)S(1)}, bf16[128,1536]{1,0:T(8,128)(2,1)}, u32[]{:S(2)}) copy-start(bf16[128,1536]{1,0:T(8,128)(2,1)} %q_ref.1) | copy-start | bytes 1179652
  2.1 1.0 %copy-start.2 = (bf16[128,1536]{1,0:T(8,128)(2,1)S(1)}, bf16[128,1536]{1,0:T(8,128)(2,1)}, u32[]{:S(2)}) copy-start(bf16[128,1536]{1,0:T(8,128)(2,1)} %k_ref.1) | copy-start | bytes 1179652
  3.1 1.0 %copy-start.3 = (bf16[128,1536]{1,0:T(8,128)(2,1)S(1)}, bf16[128,1536]{1,0:T(8,128)(2,1)}, u32[]{:S(2)}) copy-start(bf16[128,1536]{1,0:T(8,128)(2,1)} %v_ref.1) | copy-start | bytes 1179652
  4.1 0.9 %copy-start.4 = (f32[8,3072]{1,0:T(8,128)S(1)}, f32[8,3072]{1,0:T(8,128)}, u32[]{:S(2)}) copy-start(f32[8,3072]{1,0:T(8,128)} %gate_ref.1) | copy-start | bytes 294916
  5.0 0.7 copy-start.5
  5.7 0.7 copy-start.6

commit v2 on v1

--- a/solution.py
+++ b/solution.py
@@ -18,15 +18,21 @@
 def kernel(
     n,
     slots,
+    q_hbm,
+    k_hbm,
+    v_hbm,
+    dest_hbm,
+    clip_hbm,
+    gate_hbm,
+    residual_hbm,
+    weight_hbm,
+    out_ref,
     q_ref,
     k_ref,
     v_ref,
     dest_ref,
     clip_ref,
     gate_ref,
-    residual_hbm,
-    weight_hbm,
-    out_ref,
     send,
     recv,
     meta_send,
@@ -59,6 +65,14 @@
     mine = me % GROUP
 
     barrier = pltpu.get_barrier_semaphore()
+    sources = (dest_hbm, clip_hbm, q_hbm, k_hbm, v_hbm, gate_hbm, residual_hbm, weight_hbm)
+    targets = (dest_ref, clip_ref, q_ref, k_ref, v_ref, gate_ref, residual, weight)
+    loads = [
+        pltpu.make_async_copy(source, target, load_sem.at[i])
+        for i, (source, target) in enumerate(zip(sources, targets))
+    ]
+    for load in loads[:5]:
+        load.start()
 
     def greet(o, carry):
         pl.semaphore_signal(barrier, inc=1, device_id=((me + o) % n,), device_id_type=MESH)
@@ -66,9 +80,8 @@
 
     lax.fori_loop(1, n, greet, 0)
 
-    load_weight = pltpu.make_async_copy(weight_hbm, weight, load_sem.at[0])
-    load_residual = pltpu.make_async_copy(residual_hbm, residual, load_sem.at[1])
-
+    loads[0].wait()
+    loads[1].wait()
     dest_row = dest_ref[...]
     win_row = lax.div(dest_row, jnp.int32(window))
     code_row = lax.rem(dest_row, jnp.int32(window)) + 1 + clip_ref[...] * 1024
@@ -153,6 +166,8 @@
 
     for c in range(chunks):
         for t, ref in enumerate((q_ref, k_ref, v_ref)):
+            if c == 0:
+                loads[2 + t].wait()
             packed = jnp.dot(
                 place, ref[:, c * wide : (c + 1) * wide], preferred_element_type=F32
             ).astype(BF16)
@@ -164,22 +179,23 @@
         if c == 0:
             pl.semaphore_wait(barrier, n - 1)
 
-            def start_meta(i, carry):
-                meta_copy(order(i)).start()
-                return carry
-
-            lax.fori_loop(0, n - 1, start_meta, 0)
-            own_meta.start()
-
         def start_chunk(i, carry, c=c):
             copy(c, order(i)).start()
             return carry
 
         lax.fori_loop(0, n - 1, start_chunk, 0)
         own_copy(c).start()
-
-    load_weight.start()
-    load_residual.start()
+        if c == 0:
+
+            def start_meta(o, carry):
+                meta_copy(o).start()
+                return carry
+
+            lax.fori_loop(1, n, start_meta, 0)
+            own_meta.start()
+
+    for load in loads[5:]:
+        load.start()
 
     def wait_meta(o, carry):
         meta_arrival(o).wait_recv()
@@ -216,6 +232,7 @@
                 query_clip == key_clip, 0.0, -1e30
             )
 
+    loads[5].wait()
     clips = gate_ref.shape[0]
     my_clip = clip_col[pl.ds(pl.multiple_of(mine * tile, tile), tile), :]
     lookup = jnp.where(
@@ -229,8 +246,8 @@
             precision=lax.Precision.HIGHEST,
             preferred_element_type=F32,
         )
-    load_weight.wait()
-    load_residual.wait()
+    loads[6].wait()
+    loads[7].wait()
 
     def back_copy(c, o):
         to = (mine + o) % GROUP
@@ -334,14 +351,20 @@
     slots = max(GROUP * (2 * tile // n), 16)
     window = GROUP * tile
     vmem = pl.BlockSpec(memory_space=pltpu.VMEM)
-    anywhere = pl.BlockSpec(memory_space=pl.ANY)
+    anywhere = pl.BlockSpec(memory_space=pltpu.HBM)
     dma = pltpu.SemaphoreType.DMA
     return pl.pallas_call(
         functools.partial(kernel, n, slots),
         out_shape=jax.ShapeDtypeStruct((tile, width), BF16),
-        in_specs=[vmem] * 6 + [anywhere] * 2,
+        in_specs=[anywhere] * 8,
         out_specs=vmem,
         scratch_shapes=[
+            pltpu.VMEM((tile, features), BF16),
+            pltpu.VMEM((tile, features), BF16),
+            pltpu.VMEM((tile, features), BF16),
+            pltpu.VMEM((1, tile), jnp.int32),
+            pltpu.VMEM((1, tile), jnp.int32),
+            pltpu.VMEM(gate.shape, F32),
             pltpu.VMEM((chunks, windows, GROUP, slots, 3 * HEAD_DIM), BF16),
             pltpu.VMEM((chunks, n, slots, 3 * HEAD_DIM), BF16),
             pltpu.VMEM((windows, 1, 128), jnp.int32),
@@ -361,11 +384,11 @@
             dma((n,)),
             dma((chunks, GROUP)),
             dma((chunks, GROUP)),
-            dma((2,)),
+            dma((8,)),
             dma((2 * chunks + 1,)),
         ],
         compiler_params=pltpu.CompilerParams(
-            collective_id=0, has_side_effects=True, vmem_limit_bytes=50 * 1024 * 1024
+            collective_id=0, has_side_effects=True, vmem_limit_bytes=60 * 1024 * 1024
         ),
     )(
         queries,

time: 74 us -> 69.6 us (0.941)
  local copies, waits for them, and re-layouts: 7.2 us -> 2.06 us
  Pallas kernels: 66.5 us -> 67.3 us
    unnamed x15 -> x1, local copies, waits for them, and re-layouts: 7.2 us -> 2.06 us
    pallas_call x1, Pallas kernels: 66.5 us -> 67.3 us  [shards(): pl.pallas_call(functools.partial(kernel, n, slots), out_shape=jax.ShapeDt...]
where the time goes in v2:
time: 69.6 us; the launch traced here: 69.4 us
  Pallas kernels  67.3 us (97%)
  local copies, waits for them, and re-layouts  2.06 us (3%)
    pallas_call x1, Pallas kernels, shards(): pl.pallas_call(functools.partial(kernel, n, slots), out_shape=jax.ShapeDt...  67.3 us
    unnamed x1, local copies, waits for them, and re-layouts  2.06 us

profile of v2, /device:TPU:13, one launch (start us, length us, event | category | flops | bytes accessed | tf_op | source)
XLA Modules:
  0.0 69.4 jit_solution(11684068859195043824)
XLA Ops:
  0.0 67.3 %shard_map.82 = bf16[128,3072]{1,0:T(8,128)(2,1)} custom-call(bf16[128,1536]{1,0:T(8,128)(2,1)} %q_hbm.1, bf16[128,1536]{1,0:T(8,128)(2,1)} %k_hbm.1, bf16[128,1536]{1,0:T(8,128)(2,1)} %v_hbm.1, s32[1,128]{1,0:T(1,128)} %bitcast.2, s32[1,128]{1,0:T(1,128)} %bitcast.3, f32[8,3072]{1,0:T(8,128)} %gate_hbm.1, bf16[128,3072]{1,0:T(8,128)(2,1)} %residual_hbm.1, ...), custom_call_target="tpu_custom_call" | custom-call | tf_op jit(solution)/shard_map/pallas_call | solution.py:356
  67.3 2.1 %copy.10 = bf16[128,3072]{1,0:T(8,128)(2,1)} copy(bf16[128,3072]{1,0:T(8,128)(2,1)} %shard_map.82) | data formatting | bytes 1572864

commit v3 on v2

--- a/solution.py
+++ b/solution.py
@@ -26,7 +26,7 @@
     gate_hbm,
     residual_hbm,
     weight_hbm,
-    out_ref,
+    out_hbm,
     q_ref,
     k_ref,
     v_ref,
@@ -46,6 +46,8 @@
     gate_rows,
     weight,
     residual,
+    out_ref,
+    store_sem,
     send_sem,
     recv_sem,
     meta_send_sem,
@@ -110,9 +112,6 @@
     slot_line = lax.broadcasted_iota(jnp.int32, (windows * slots, tile), 0)
     place = jnp.where(slot_line == slot_row, 1.0, 0.0).astype(BF16)
 
-    def order(i):
-        return n // 2 + (1 - 2 * (i % 2)) * ((i + 1) // 2)
-
     def meta_copy(o):
         to = (me + o) % n
         return pltpu.make_async_remote_copy(
@@ -180,10 +179,10 @@
             pl.semaphore_wait(barrier, n - 1)
 
         def start_chunk(i, carry, c=c):
-            copy(c, order(i)).start()
+            copy(c, i).start()
             return carry
 
-        lax.fori_loop(0, n - 1, start_chunk, 0)
+        lax.fori_loop(1, n, start_chunk, 0)
         own_copy(c).start()
         if c == 0:
 
@@ -271,6 +270,11 @@
             device_id_type=MESH,
         )
 
+    def store(x):
+        return pltpu.make_async_copy(
+            out_ref.at[:, x : x + 512], out_hbm.at[:, x : x + 512], store_sem.at[x // 512]
+        )
+
     def project(c):
         for o in range(1, GROUP):
             back_arrival(c, o).wait_recv()
@@ -290,6 +294,7 @@
                 out_ref[:, x : x + 512] = (
                     residual[:, x : x + 512].astype(F32) + gate_rows[:, x : x + 512] * part
                 ).astype(out_ref.dtype)
+                store(x).start()
 
     def own_back(c):
         return pltpu.make_async_copy(
@@ -337,6 +342,8 @@
         return carry
 
     lax.fori_loop(1, n, wait_sent, 0)
+    for x in range(0, width, 512):
+        store(x).wait()
     for c in range(chunks):
         for o in range(1, GROUP):
             back_copy(c, o).wait_send()
@@ -350,14 +357,13 @@
     windows = n // GROUP
     slots = max(GROUP * (2 * tile // n), 16)
     window = GROUP * tile
-    vmem = pl.BlockSpec(memory_space=pltpu.VMEM)
     anywhere = pl.BlockSpec(memory_space=pltpu.HBM)
     dma = pltpu.SemaphoreType.DMA
     return pl.pallas_call(
         functools.partial(kernel, n, slots),
         out_shape=jax.ShapeDtypeStruct((tile, width), BF16),
         in_specs=[anywhere] * 8,
-        out_specs=vmem,
+        out_specs=anywhere,
         scratch_shapes=[
             pltpu.VMEM((tile, features), BF16),
             pltpu.VMEM((tile, features), BF16),
@@ -378,6 +384,8 @@
             pltpu.VMEM((tile, width), F32),
             pltpu.VMEM((features, width), BF16),
             pltpu.VMEM((tile, width), BF16),
+            pltpu.VMEM((tile, width), BF16),
+            dma((width // 512,)),
             dma((chunks, n)),
             dma((chunks, n)),
             dma((n,)),

time: 69.6 us -> 69.2 us (level)
  no operation moved by 1% of the time
where the time goes in v3:
time: 69.2 us; the launch traced here: 69.1 us
  Pallas kernels  67 us (97%)
  local copies, waits for them, and re-layouts  2.06 us (3%)
    pallas_call x1, Pallas kernels, shards(): pl.pallas_call(functools.partial(kernel, n, slots), out_shape=jax.ShapeDt...  67 us
    unnamed x1, local copies, waits for them, and re-layouts  2.06 us

profile of v3, /device:TPU:13, one launch (start us, length us, event | category | flops | bytes accessed | tf_op | source)
XLA Modules:
  0.0 69.1 jit_solution(14854260074899999972)
XLA Ops:
  0.0 67.0 %shard_map.82 = bf16[128,3072]{1,0:T(8,128)(2,1)} custom-call(bf16[128,1536]{1,0:T(8,128)(2,1)} %q_hbm.1, bf16[128,1536]{1,0:T(8,128)(2,1)} %k_hbm.1, bf16[128,1536]{1,0:T(8,128)(2,1)} %v_hbm.1, s32[1,128]{1,0:T(1,128)} %bitcast.2, s32[1,128]{1,0:T(1,128)} %bitcast.3, f32[8,3072]{1,0:T(8,128)} %gate_hbm.1, bf16[128,3072]{1,0:T(8,128)(2,1)} %residual_hbm.1, ...), custom_call_target="tpu_custom_call" | custom-call | tf_op jit(solution)/shard_map/pallas_call | solution.py:362
  67.0 2.1 %copy.10 = bf16[128,3072]{1,0:T(8,128)(2,1)} copy(bf16[128,3072]{1,0:T(8,128)(2,1)} %shard_map.82) | data formatting | bytes 1572864
